TPU v7x, 512 devices: a whole 4x8x8 slice. The times are simulated.
512 devices in a mesh: dp: 8 (over y), ta: 16 (over z_lo, x), ha: 4 (over z_hi, core).
Axes of the slice: x: 4, y: 8, z: 8 (z_hi: 2, z_lo: 4; z = z_hi * 4 + z_lo), core: 2. Of those that a mesh axis runs over, the one named last changes fastest.
Arguments:
- decoder_feature_rows: bfloat16 [32768, 768], P(('dp', 'ta', 'ha')), parts along dimension 0, may hold values from -12 to 12
- slot_row_index: int32 [32768], P('dp'), parts along dimension 0, may hold values from 0 to 4095, as said below
- latent_frame_count: int32 [48], P('dp'), parts along dimension 0, may hold values from 1 to 81, 256 in all
- first_norm_gain: float32 [384], replicated, may hold values from 0.1 to 1.9
- first_norm_bias: float32 [384], replicated, may hold values from -3 to 3
- first_convolution_weight: bfloat16 [3, 3, 3, 384, 384], P(None, None, None, 'ha'), may hold values from -0.0625 to 0.0625
- first_convolution_bias: float32 [384], replicated, may hold values from -3 to 3
- second_norm_gain: float32 [384], replicated, may hold values from 0.1 to 1.9
- second_norm_bias: float32 [384], replicated, may hold values from -3 to 3
- second_convolution_weight: bfloat16 [3, 3, 3, 384, 384], P(None, None, None, 'ha'), may hold values from -0.0625 to 0.0625
- second_convolution_bias: float32 [384], replicated, may hold values from -3 to 3
Outputs:
- decoded: bfloat16 [2048, 16, 2, 384], P(('dp', 'ta'), 'ha'), parts along dimension 0
There are 8 independent parts, one for each index of `dp`. A program takes and returns all parts, laid end to end along the dimension named above; an argument that names none is the same for every part. Nothing has to cross between parts.
Inputs may be any that keep to these rules, and one draw needn't show every extreme that they name: `slot_row_index`: A permutation of 0 to 4095. Slot i lies on the device of flat index i // 64 over ta+ha; row g is owned by the device of ta index (g // 16) // 16 and ha index (g % 16) // 4. The slots of one device hold at most 2 rows of any one owner, and exactly 2 of some owner.
All inputs are finite; a program needn't handle non-finite values.
Results may differ from a plain program's by a relative error of at most 0.0042.
Values may be sent and summed in bfloat16 or wider, within the bound.
No kernel may reach another device: no remote copies, remote signals or barrier semaphores. Data moves between devices by JAX's collectives and lax.ppermute only.
A program may use at most 64 MiB of HBM per device.

v0:
```python
import jax
import jax.numpy as jnp
from jax import lax
from jax.sharding import PartitionSpec as P

CH = 384
GROUPS = 32
F_DEV = 16
R_DEV = 4
COLS = 2


def from_behind(value, axis, by):
    length = lax.axis_size(axis)
    pairs = [(i, i + by) for i in range(length) if 0 <= i + by < length]
    return lax.ppermute(value, axis, pairs)


def group_sums(values, groups):
    extent = values.shape
    grouped = values.reshape(extent[0], extent[1] * extent[2], groups, extent[3] // groups)
    return (jnp.sum(grouped, axis=(1, 3)), jnp.sum(grouped * grouped, axis=(1, 3)))


def normalize(values, totals, squares, entries, gain_vec, offset, groups):
    average = totals / entries
    spread = squares / entries - average * average
    inverse = lax.rsqrt(spread + 1e-06)
    extent = values.shape
    grouped = values.reshape(extent[0], extent[1], extent[2], groups, extent[3] // groups)
    centred = (grouped - average[:, None, None, :, None]) * inverse[:, None, None, :, None]
    scaled = centred.reshape(extent) * gain_vec + offset
    return jax.nn.silu(scaled).astype(jnp.bfloat16)


def extend_frames(values):
    earlier = from_behind(values[-2:], "ta", 1)
    return jnp.concatenate([earlier, values], axis=0)


def whole_rows(values):
    return lax.all_gather(values, "ha", axis=1, tiled=True)


def shared_norm(values, gain_vec, offset, entries):
    part_sums, part_squares = group_sums(values, GROUPS)
    totals, squares = lax.psum((part_sums, part_squares), "ha")
    return normalize(values, totals, squares, entries, gain_vec, offset, GROUPS)


def causal_conv(extended, weight, masks):
    frames = extended.shape[0] - 2
    image_height = extended.shape[1]
    columns = extended.shape[2]
    channels = extended.shape[3]
    outputs = weight.shape[3]
    padded = jnp.pad(extended, ((0, 0), (1, 1), (1, 1), (0, 0)))
    stacked = jnp.concatenate(
        [
            padded[time_tap : time_tap + frames] * masks[time_tap][:, None, None, None]
            for time_tap in range(3)
        ],
        axis=3,
    )
    kernel = jnp.transpose(weight, (0, 4, 1, 2, 3)).reshape(3 * channels, 9 * outputs)
    taps = jnp.dot(stacked.reshape(-1, 3 * channels), kernel, preferred_element_type=jnp.float32)
    taps = taps.reshape(frames, image_height + 2, columns + 2, 9, outputs)
    total = jnp.zeros((frames, image_height, columns, outputs), jnp.float32)
    for row_tap in range(3):
        for col_tap in range(3):
            total = (
                total
                + taps[
                    :,
                    row_tap : row_tap + image_height,
                    col_tap : col_tap + columns,
                    3 * row_tap + col_tap,
                ]
            )
    return total


def rearrange_rows(decoder_feature_rows, slot_row_index, image_height):
    devices = lax.axis_size(("ta", "ha"))
    ha_count = lax.axis_size("ha")
    number_of_slots = decoder_feature_rows.shape[0]
    capacity = number_of_slots // devices + 1
    own_index = lax.axis_index(("ta", "ha"))
    plan_grid = slot_row_index.reshape(devices, number_of_slots)
    frame_of = plan_grid // image_height
    row_in = plan_grid % image_height
    owners = frame_of // F_DEV * ha_count + row_in // R_DEV
    places = frame_of % F_DEV * R_DEV + row_in % R_DEV
    my_owners = lax.dynamic_slice_in_dim(owners, own_index, 1, 0)[0]
    matches = (my_owners[:, None] == jnp.arange(devices, dtype=jnp.int32)[None, :]).astype(
        jnp.int32
    )
    ranking = jnp.sum((jnp.cumsum(matches, axis=0) - 1) * matches, axis=1)
    position = my_owners * capacity + ranking
    row_packing = (
        jnp.arange(devices * capacity, dtype=jnp.int32)[:, None] == position[None, :]
    ).astype(jnp.bfloat16)
    departing_rows = jnp.dot(
        row_packing, decoder_feature_rows, preferred_element_type=jnp.float32
    ).astype(jnp.bfloat16)
    incoming = lax.all_to_all(
        departing_rows.reshape(devices, capacity, -1),
        ("ta", "ha"),
        split_axis=0,
        concat_axis=0,
        tiled=True,
    )
    arrivals = (owners == own_index).astype(jnp.int32)
    order_in = jnp.cumsum(arrivals, axis=1) - 1
    chosen = arrivals[:, None, :] * (
        order_in[:, None, :] == jnp.arange(capacity, dtype=jnp.int32)[None, :, None]
    ).astype(jnp.int32)
    filled = jnp.sum(chosen, axis=2)
    target = jnp.sum(chosen * places[:, None, :], axis=2) + filled - 1
    unpack = (
        jnp.arange(number_of_slots, dtype=jnp.int32)[:, None] == target.reshape(1, -1)
    ).astype(jnp.bfloat16)
    placed = jnp.dot(
        unpack, incoming.reshape(devices * capacity, -1), preferred_element_type=jnp.float32
    )
    return placed.astype(jnp.bfloat16).reshape(F_DEV, R_DEV, COLS, CH)


def local(
    decoder_feature_rows,
    slot_row_index,
    latent_frame_count,
    first_norm_gain,
    first_norm_bias,
    first_convolution_weight,
    first_convolution_bias,
    second_norm_gain,
    second_norm_bias,
    second_convolution_weight,
    second_convolution_bias,
):
    ha_count = lax.axis_size("ha")
    ha_index = lax.axis_index("ha")
    image_height = R_DEV * ha_count
    out_width = CH // ha_count
    latent_row_list = rearrange_rows(decoder_feature_rows, slot_row_index, image_height)
    frame_ids = lax.axis_index("ta") * F_DEV + jnp.arange(F_DEV, dtype=jnp.int32)
    video_ends = jnp.cumsum(latent_frame_count)
    starts = jnp.sum(
        jnp.where(video_ends[None, :] <= frame_ids[:, None], latent_frame_count[None, :], 0), axis=1
    )
    masks = jnp.stack([frame_ids - 2 + time_tap >= starts for time_tap in range(3)]).astype(
        jnp.bfloat16
    )
    bias_first = lax.dynamic_slice_in_dim(first_convolution_bias, ha_index * out_width, out_width)
    bias_second = lax.dynamic_slice_in_dim(second_convolution_bias, ha_index * out_width, out_width)
    entries = image_height * COLS * (CH // GROUPS)
    latent_float = latent_row_list.astype(jnp.float32)
    first_act = shared_norm(latent_float, first_norm_gain, first_norm_bias, entries)
    hidden = (
        causal_conv(whole_rows(extend_frames(first_act)), first_convolution_weight, masks)
        + bias_first
    ).astype(jnp.bfloat16)
    hidden_rows = lax.all_to_all(hidden, "ha", split_axis=1, concat_axis=3, tiled=True)
    second_act = shared_norm(
        hidden_rows.astype(jnp.float32), second_norm_gain, second_norm_bias, entries
    )
    result = (
        causal_conv(whole_rows(extend_frames(second_act)), second_convolution_weight, masks)
        + bias_second
    )
    output_rows = lax.all_to_all(result, "ha", split_axis=1, concat_axis=3, tiled=True)
    return (output_rows + latent_float).astype(jnp.bfloat16)


def solution(mesh):
    in_specs = (
        P(("dp", "ta", "ha"), None),
        P("dp"),
        P("dp"),
        P(),
        P(),
        P(None, None, None, "ha", None),
        P(),
        P(),
        P(),
        P(None, None, None, "ha", None),
        P(),
    )
    out_specs = P(("dp", "ta"), "ha", None, None)
    return jax.shard_map(local, mesh=mesh, in_specs=in_specs, out_specs=out_specs, check_vma=False)
```

profile of v0, /device:TPU:112, one launch (start us, length us, event | category | flops | bytes accessed | tf_op | source)
XLA Modules:
  0.0 152.8 jit_solution(9828036770972007920)
XLA Ops:
  0.0 0.8 reshape.350
  1.5 0.8 reshape.351
  2.2 13.0 %all-to-all-start = ((bf16[64,2,768]{2,1,0:T(2,128)(2,1)}), bf16[64,2,768]{2,1,0:T(2,128)(2,1)S(1)}, u32[]{:S(2)}, u32[]{:S(2)}) async-start(bf16[64,2,768]{2,1,0:T(2,128)(2,1)} %reshape.351), calls=%async_computation | async-start | bytes 393216 | tf_op jit(solution)/shard_map/all_to_all | solution.py:106
  15.6 0.8 reduce-window.8
  16.5 0.7 select_reduce_fusion.2
  17.6 9.4 %all-to-all-done = bf16[64,2,768]{2,1,0:T(2,128)(2,1)S(1)} async-done(((bf16[64,2,768]{2,1,0:T(2,128)(2,1)}), bf16[64,2,768]{2,1,0:T(2,128)(2,1)S(1)}, u32[]{:S(2)}, u32[]{:S(2)}) %all-to-all-start) | async-done | bytes 196640 | tf_op jit(solution)/shard_map/all_to_all | solution.py:106
  27.2 2.3 %reshape.358 = f32[16,8,32,12]{3,2,1,0:T(8,128)S(1)} reshape(f32[64,768]{1,0:T(8,128)S(1)} %fusion.16) | data formatting | bytes 393216 | tf_op jit(solution)/shard_map/convert_element_type | solution.py:158
  30.1 19.1 %all-reduce.3 = (f32[16,32]{1,0:T(8,128)S(1)}, f32[16,32]{1,0:T(8,128)S(1)}) all-reduce(f32[16,32]{1,0:T(8,128)S(1)} %get-tuple-element.6, f32[16,32]{1,0:T(8,128)S(1)} %get-tuple-element.5), channel_id=1, replica_groups=mesh['dp'=8,'ta'=16,'ha'=4] {'ha'}, use_global_device_ids=true, to_apply=%region_8.9 | all-reduce | flops 1024 | bytes 8192 | tf_op jit(solution)/shard_map/psum | solution.py:47
  49.9 2.4 %collective-permute-start = (bf16[2,4,2,384]{3,0,2,1:T(2,128)(2,1)S(1)}, bf16[2,4,2,384]{3,0,2,1:T(2,128)(2,1)S(1)}, u32[]{:S(2)}, u32[]{:S(2)}) collective-permute-start(bf16[2,4,2,384]{3,0,2,1:T(2,128)(2,1)S(1)} %slice.119), channel_id=1, source_target_pairs={{0,4},{4,8},{8,12},{12,16},{16,20},{20,24},{24,28},{28,32},{32,36}... | collective-permute-start | bytes 36872 | tf_op jit(solution)/shard_map/ppermute | solution.py:16
  52.4 2.9 %copy.55 = bf16[3,384,3,3,96]{1,0,4,3,2:T(4,128)(2,1)S(1)} copy(bf16[3,384,3,3,96]{1,4,3,2,0:T(8,128)(2,1)} %bitcast.90) | data formatting | bytes 3981312 | tf_op jit(solution)/shard_map/transpose | solution.py:65
  55.7 0.8 dynamic_slice.10
  56.5 1.2 collective-permute-done
  57.8 11.8 %all_gather.6 = bf16[18,16,2,384]{3,2,0,1:T(2,128)(2,1)S(1)} all-gather(bf16[18,4,2,384]{3,2,0,1:T(2,128)(2,1)S(1)} %copy.53), channel_id=1, replica_groups=mesh['dp'=8,'ta'=16,'ha'=4] {'ha'}, dimensions={1}, use_global_device_ids=true | all-gather | bytes 552960 | tf_op jit(solution)/shard_map/all_gather | solution.py:42
  70.0 5.5 %fusion = f32[16,18,4,9,96]{4,1,3,2,0:T(8,128)S(1)} fusion(bf16[9,96,1152,1,1]{2,1,0,4,3:T(8,128)(2,1)S(1)} %bitcast.92, bf16[16,18,4,384]{3,1,2,0:T(8,128)(2,1)S(1)} %get-tuple-element.22, bf16[16,18,4,384]{3,1,2,0:T(8,128)(2,1)S(1)} %get-tuple-element.21, bf16[16,18,4,384]{3,1,2,0:T(8,128)(2,1)S(1)} %get-tuple-element.20), kind=kOutput, calls=%fused_computation.1 | convolution fusion | flops 2301198336 | bytes 8626176 | tf_op jit(solution)/shard_map/dot_general | solution.py:66
  75.8 12.6 %all_to_all.32 = bf16[16,16,2,96]{3,2,0,1:T(2,128)(2,1)S(1)} all-to-all(bf16[16,16,2,96]{3,2,0,1:T(2,128)(2,1)S(1)} %copy.56), channel_id=1, replica_groups=mesh['dp'=8,'ta'=16,'ha'=4] {'ha'}, dimensions={1} | all-to-all | bytes 196608 | tf_op jit(solution)/shard_map/all_to_all | solution.py:164
  89.6 18.0 %all-reduce.2 = (f32[16,32]{1,0:T(8,128)S(1)}, f32[16,32]{1,0:T(8,128)S(1)}) all-reduce(f32[16,32]{1,0:T(8,128)S(1)} %reduce_sum.103, f32[16,32]{1,0:T(8,128)S(1)} %reduce_sum.100), channel_id=1, replica_groups=mesh['dp'=8,'ta'=16,'ha'=4] {'ha'}, use_global_device_ids=true, to_apply=%region_16.17 | all-reduce | flops 1024 | bytes 8192 | tf_op jit(solution)/shard_map/psum | solution.py:47
  108.5 1.9 %collective-permute-start.1 = (bf16[2,4,2,384]{3,0,2,1:T(2,128)(2,1)S(1)}, bf16[2,4,2,384]{3,0,2,1:T(2,128)(2,1)S(1)}, u32[]{:S(2)}, u32[]{:S(2)}) collective-permute-start(bf16[2,4,2,384]{3,0,2,1:T(2,128)(2,1)S(1)} %slice.129), channel_id=1, source_target_pairs={{0,4},{4,8},{8,12},{12,16},{16,20},{20,24},{24,28},{28,32},{32,36}... | collective-permute-start | bytes 36872 | tf_op jit(solution)/shard_map/ppermute | solution.py:16
  110.4 1.4 copy.60
  112.2 0.8 dynamic_slice.11
  112.9 3.2 %collective-permute-done.1 = bf16[2,4,2,384]{3,0,2,1:T(2,128)(2,1)S(1)} collective-permute-done((bf16[2,4,2,384]{3,0,2,1:T(2,128)(2,1)S(1)}, bf16[2,4,2,384]{3,0,2,1:T(2,128)(2,1)S(1)}, u32[]{:S(2)}, u32[]{:S(2)}) %collective-permute-start.1) | collective-permute-done | bytes 12320 | tf_op jit(solution)/shard_map/ppermute | solution.py:16
  116.3 12.8 %all_gather.7 = bf16[18,16,2,384]{3,2,0,1:T(2,128)(2,1)S(1)} all-gather(bf16[18,4,2,384]{3,2,0,1:T(2,128)(2,1)S(1)} %copy.58), channel_id=1, replica_groups=mesh['dp'=8,'ta'=16,'ha'=4] {'ha'}, dimensions={1}, use_global_device_ids=true | all-gather | bytes 552960 | tf_op jit(solution)/shard_map/all_gather | solution.py:42
  129.6 5.4 %fusion.5 = f32[16,18,4,9,96]{4,1,3,2,0:T(8,128)S(1)} fusion(bf16[9,96,1152,1,1]{2,1,0,4,3:T(8,128)(2,1)S(1)} %bitcast.93, bf16[16,18,4,384]{3,1,2,0:T(8,128)(2,1)S(1)} %get-tuple-element.19, bf16[16,18,4,384]{3,1,2,0:T(8,128)(2,1)S(1)} %get-tuple-element.18, bf16[16,18,4,384]{3,1,2,0:T(8,128)(2,1)S(1)} %get-tuple-element.17), kind=kOutput, calls=%fused_computation.7 | convolution fusion | flops 2301198336 | bytes 8626176 | tf_op jit(solution)/shard_map/dot_general | solution.py:66
  135.3 16.3 %all_to_all.33 = f32[16,16,2,96]{3,2,0,1:T(2,128)S(1)} all-to-all(f32[16,16,2,96]{3,2,0,1:T(2,128)S(1)} %copy.61), channel_id=1, replica_groups=mesh['dp'=8,'ta'=16,'ha'=4] {'ha'}, dimensions={1} | all-to-all | bytes 393216 | tf_op jit(solution)/shard_map/all_to_all | solution.py:172
  152.1 0.7 add_convert_fusion
  (71 shorter events, 7.9 us)
Async XLA Ops:
  0.0 1.3 copy-start
  2.2 24.7 %all-to-all-start = ((bf16[64,2,768]{2,1,0:T(2,128)(2,1)}), bf16[64,2,768]{2,1,0:T(2,128)(2,1)S(1)}, u32[]{:S(2)}, u32[]{:S(2)}) async-start(bf16[64,2,768]{2,1,0:T(2,128)(2,1)} %reshape.351), calls=%async_computation | async-start | bytes 393216 | tf_op jit(solution)/shard_map/all_to_all | solution.py:106
  29.5 20.3 %copy-start.2 = (f32[384]{0:T(512)S(1)}, f32[384]{0:T(512)}, u32[]{:S(2)}) copy-start(f32[384]{0:T(512)} %param.15) | copy-start | bytes 4612
  29.5 20.3 %copy-start.3 = (f32[384]{0:T(512)S(1)}, f32[384]{0:T(512)}, u32[]{:S(2)}) copy-start(f32[384]{0:T(512)} %param.14) | copy-start | bytes 4612
  49.9 7.7 %collective-permute-start = (bf16[2,4,2,384]{3,0,2,1:T(2,128)(2,1)S(1)}, bf16[2,4,2,384]{3,0,2,1:T(2,128)(2,1)S(1)}, u32[]{:S(2)}, u32[]{:S(2)}) collective-permute-start(bf16[2,4,2,384]{3,0,2,1:T(2,128)(2,1)S(1)} %slice.119), channel_id=1, source_target_pairs={{0,4},{4,8},{8,12},{12,16},{16,20},{20,24},{24,28},{28,32},{32,36}... | collective-permute-start | bytes 36872 | tf_op jit(solution)/shard_map/ppermute | solution.py:16
  88.4 19.9 %copy-start.4 = (f32[384]{0:T(512)S(1)}, f32[384]{0:T(512)}, u32[]{:S(2)}) copy-start(f32[384]{0:T(512)} %param.19) | copy-start | bytes 4612
  88.4 19.9 %copy-start.5 = (f32[384]{0:T(512)S(1)}, f32[384]{0:T(512)}, u32[]{:S(2)}) copy-start(f32[384]{0:T(512)} %param.18) | copy-start | bytes 4612
  88.6 21.8 %copy-start.1 = (bf16[3,3,3,96,384]{4,3,2,1,0:T(8,128)(2,1)S(1)}, bf16[3,3,3,96,384]{4,3,2,1,0:T(8,128)(2,1)}, u32[]{:S(2)}) copy-start(bf16[3,3,3,96,384]{4,3,2,1,0:T(8,128)(2,1)} %param.20) | copy-start | bytes 5971972
  108.5 7.7 %collective-permute-start.1 = (bf16[2,4,2,384]{3,0,2,1:T(2,128)(2,1)S(1)}, bf16[2,4,2,384]{3,0,2,1:T(2,128)(2,1)S(1)}, u32[]{:S(2)}, u32[]{:S(2)}) collective-permute-start(bf16[2,4,2,384]{3,0,2,1:T(2,128)(2,1)S(1)} %slice.129), channel_id=1, source_target_pairs={{0,4},{4,8},{8,12},{12,16},{16,20},{20,24},{24,28},{28,32},{32,36}... | collective-permute-start | bytes 36872 | tf_op jit(solution)/shard_map/ppermute | solution.py:16
where the time goes:
time: 153 us
  blocking collectives  90.5 us (59%)
  starting transfers between devices  17.4 us (11%)
  waiting for transfers between devices  13.8 us (9%)
  local copies, waits for them, and re-layouts  13.7 us (9%)
  matrix products  11.2 us (7%)
  other arithmetic  5.8 us (4%)
    psum x2, blocking collectives, shared_norm(): totals, squares = lax.psum((part_sums, part_squares), 'ha')  37 us
    all_gather x2, blocking collectives, whole_rows(): return lax.all_gather(values, 'ha', axis=1, tiled=True)  24.6 us
    all_to_all x1, blocking collectives, local(): lax.all_to_all(result, 'ha', split_axis=1, concat_axis=3, tiled=True)  16.3 us
    all_to_all x1, starting transfers between devices, rearrange_rows(): lax.all_to_all(departing_rows.reshape(devices, capacity, -1), ('ta', 'ha'...  13 us
    all_to_all x1, blocking collectives, local(): lax.all_to_all(hidden, 'ha', split_axis=1, concat_axis=3, tiled=True)  12.6 us
    dot_general x2, matrix products, causal_conv(): jnp.dot(stacked.reshape(-1, 3 * channels), kernel, preferred_element_type...  10.8 us
    all_to_all x1, waiting for transfers between devices, rearrange_rows(): lax.all_to_all(departing_rows.reshape(devices, capacity, -1), ('ta', 'ha'...  9.42 us
    ppermute x2, waiting for transfers between devices, from_behind(): return lax.ppermute(value, axis, pairs)  4.42 us
  transfers between devices with their start and end apart: 3, of which 3 were waited for; matrix products, arithmetic and copies ran while one was open for 6% of the time, Pallas kernels for 0%

commit v1 on v0

--- a/solution.py
+++ b/solution.py
@@ -39,7 +39,14 @@
 
 
 def whole_rows(values):
-    return lax.all_gather(values, "ha", axis=1, tiled=True)
+
+    def cycles_hold(matrix):
+        b_now = tuple((matrix for _ in range(lax.axis_size("ha"))))
+        part_next = jnp.stack(b_now, axis=0)
+        outcome_arr = lax.all_to_all(part_next, axis_name="ha", split_axis=0, concat_axis=0)
+        return jnp.concatenate(outcome_arr, axis=1)
+
+    return cycles_hold(values)
 
 
 def shared_norm(values, gain_vec, offset, entries):

time: 153 us -> 174 us (1.14)
  waiting for transfers between devices: 13.8 us -> 46.4 us
  blocking collectives: 90.5 us -> 64.6 us
  starting transfers between devices: 17.4 us -> 29.3 us
  local copies, waits for them, and re-layouts: 13.7 us -> 16 us
    all_to_all x0 -> x2, waiting for transfers between devices: none -> 28.6 us  [cycles_hold(): lax.all_to_all(part_next, axis_name='ha', split_axis=0, concat_axis=0)]
    all_gather x2 -> x0, blocking collectives: 24.6 us -> none  [whole_rows(): return lax.all_gather(values, 'ha', axis=1, tiled=True)]
    all_to_all x0 -> x2, starting transfers between devices: none -> 11.9 us  [cycles_hold(): lax.all_to_all(part_next, axis_name='ha', split_axis=0, concat_axis=0)]
    ppermute x2, waiting for transfers between devices: 4.42 us -> 6.76 us  [from_behind(): return lax.ppermute(value, axis, pairs)]
    another operation x0 -> x2, local copies, waits for them, and re-layouts: none -> 1.77 us  [cycles_hold(): part_next = jnp.stack(b_now, axis=0)]
  transfers between devices with their start and end apart: 3 -> 5, of which waited for: 3 -> 5; matrix products, arithmetic and copies ran while one was open for 6% -> 4% of each run, Pallas kernels for 0% -> 0%
where the time goes in v1:
time: 174 us; the launch traced here: 173 us
  blocking collectives  64.6 us (37%)
  waiting for transfers between devices  46.4 us (27%)
  starting transfers between devices  29.3 us (17%)
  local copies, waits for them, and re-layouts  16 us (9%)
  matrix products  11.3 us (6%)
  other arithmetic  5.23 us (3%)
    psum x2, blocking collectives, shared_norm(): totals, squares = lax.psum((part_sums, part_squares), 'ha')  37.1 us
    all_to_all x2, waiting for transfers between devices, cycles_hold(): lax.all_to_all(part_next, axis_name='ha', split_axis=0, concat_axis=0)  28.6 us
    all_to_all x1, blocking collectives, local(): lax.all_to_all(result, 'ha', split_axis=1, concat_axis=3, tiled=True)  15.1 us
    all_to_all x1, starting transfers between devices, rearrange_rows(): lax.all_to_all(departing_rows.reshape(devices, capacity, -1), ('ta', 'ha'...  13 us
    all_to_all x1, blocking collectives, local(): lax.all_to_all(hidden, 'ha', split_axis=1, concat_axis=3, tiled=True)  12.3 us
    all_to_all x2, starting transfers between devices, cycles_hold(): lax.all_to_all(part_next, axis_name='ha', split_axis=0, concat_axis=0)  11.9 us
    all_to_all x1, waiting for transfers between devices, rearrange_rows(): lax.all_to_all(departing_rows.reshape(devices, capacity, -1), ('ta', 'ha'...  11 us
    dot_general x2, matrix products, causal_conv(): jnp.dot(stacked.reshape(-1, 3 * channels), kernel, preferred_element_type...  10.9 us
  transfers between devices with their start and end apart: 5, of which 5 were waited for; matrix products, arithmetic and copies ran while one was open for 4% of the time, Pallas kernels for 0%

profile of v1, /device:TPU:112, one launch (start us, length us, event | category | flops | bytes accessed | tf_op | source)
XLA Modules:
  0.0 173.2 jit_solution(14138129364510027681)
XLA Ops:
  0.0 0.8 reshape.366
  2.2 13.0 %all-to-all-start = ((bf16[64,2,768]{2,1,0:T(2,128)(2,1)}), bf16[64,2,768]{2,1,0:T(2,128)(2,1)S(1)}, u32[]{:S(2)}, u32[]{:S(2)}) async-start(bf16[64,2,768]{2,1,0:T(2,128)(2,1)} %reshape.367), calls=%async_computation | async-start | bytes 393216 | tf_op jit(solution)/shard_map/all_to_all | solution.py:113
  15.9 11.0 %all-to-all-done = bf16[64,2,768]{2,1,0:T(2,128)(2,1)S(1)} async-done(((bf16[64,2,768]{2,1,0:T(2,128)(2,1)}), bf16[64,2,768]{2,1,0:T(2,128)(2,1)S(1)}, u32[]{:S(2)}, u32[]{:S(2)}) %all-to-all-start) | async-done | bytes 196640 | tf_op jit(solution)/shard_map/all_to_all | solution.py:113
  27.2 2.3 %reshape.378 = f32[16,8,32,12]{3,2,1,0:T(8,128)S(1)} reshape(f32[64,768]{1,0:T(8,128)S(1)} %fusion.16) | data formatting | bytes 393216 | tf_op jit(solution)/shard_map/convert_element_type | solution.py:165
  30.1 19.1 %all-reduce.3 = (f32[16,32]{1,0:T(8,128)S(1)}, f32[16,32]{1,0:T(8,128)S(1)}) all-reduce(f32[16,32]{1,0:T(8,128)S(1)} %get-tuple-element.6, f32[16,32]{1,0:T(8,128)S(1)} %get-tuple-element.5), channel_id=1, replica_groups=mesh['dp'=8,'ta'=16,'ha'=4] {'ha'}, use_global_device_ids=true, to_apply=%region_8.9 | all-reduce | flops 1024 | bytes 8192 | tf_op jit(solution)/shard_map/psum | solution.py:54
  50.1 2.4 %collective-permute-start = (bf16[2,4,2,384]{3,2,1,0:T(2,128)(2,1)S(1)}, bf16[2,4,2,384]{3,2,1,0:T(2,128)(2,1)S(1)}, u32[]{:S(2)}, u32[]{:S(2)}) collective-permute-start(bf16[2,4,2,384]{3,2,1,0:T(2,128)(2,1)S(1)} %slice.119), channel_id=1, source_target_pairs={{0,4},{4,8},{8,12},{12,16},{16,20},{20,24},{24,28},{28,32},{32,36}... | collective-permute-start | bytes 36872 | tf_op jit(solution)/shard_map/ppermute | solution.py:16
  52.8 2.9 %copy.47 = bf16[3,384,3,3,96]{1,0,4,3,2:T(4,128)(2,1)S(1)} copy(bf16[3,384,3,3,96]{1,4,3,2,0:T(8,128)(2,1)} %bitcast.92) | data formatting | bytes 3981312 | tf_op jit(solution)/shard_map/transpose | solution.py:72
  56.8 1.0 collective-permute-done
  58.0 0.9 stack.6
  58.9 5.3 %all-to-all-start.1 = ((bf16[4,18,4,2,384]{4,2,3,1,0:T(4,128)(2,1)}), bf16[4,18,4,2,384]{4,2,3,1,0:T(4,128)(2,1)S(1)}, u32[]{:S(2)}, u32[]{:S(2)}) async-start(bf16[4,18,4,2,384]{4,2,3,1,0:T(4,128)(2,1)} %stack.6), calls=%async_computation.1 | async-start | bytes 884736 | tf_op jit(solution)/shard_map/all_to_all | solution.py:46
  64.3 16.4 %all-to-all-done.1 = bf16[4,18,4,2,384]{4,2,3,1,0:T(4,128)(2,1)S(1)} async-done(((bf16[4,18,4,2,384]{4,2,3,1,0:T(4,128)(2,1)}), bf16[4,18,4,2,384]{4,2,3,1,0:T(4,128)(2,1)S(1)}, u32[]{:S(2)}, u32[]{:S(2)}) %all-to-all-start.1) | async-done | bytes 442400 | tf_op jit(solution)/shard_map/all_to_all | solution.py:46
  81.4 5.5 %fusion = f32[16,18,4,9,96]{4,1,3,2,0:T(8,128)S(1)} fusion(bf16[9,96,1152,1,1]{2,1,0,4,3:T(8,128)(2,1)S(1)} %bitcast.94, bf16[16,18,4,384]{3,1,2,0:T(8,128)(2,1)S(1)} %get-tuple-element.22, bf16[16,18,4,384]{3,1,2,0:T(8,128)(2,1)S(1)} %get-tuple-element.21, bf16[16,18,4,384]{3,1,2,0:T(8,128)(2,1)S(1)} %get-tuple-element.20), kind=kOutput, calls=%fused_computation.1 | convolution fusion | flops 2301198336 | bytes 8626176 | tf_op jit(solution)/shard_map/dot_general | solution.py:73
  87.2 12.3 %all_to_all.42 = bf16[16,16,2,96]{3,2,0,1:T(2,128)(2,1)S(1)} all-to-all(bf16[16,16,2,96]{3,2,0,1:T(2,128)(2,1)S(1)} %copy.48), channel_id=1, replica_groups=mesh['dp'=8,'ta'=16,'ha'=4] {'ha'}, dimensions={1} | all-to-all | bytes 196608 | tf_op jit(solution)/shard_map/all_to_all | solution.py:171
  100.5 18.1 %all-reduce.2 = (f32[16,32]{1,0:T(8,128)S(1)}, f32[16,32]{1,0:T(8,128)S(1)}) all-reduce(f32[16,32]{1,0:T(8,128)S(1)} %reduce_sum.103, f32[16,32]{1,0:T(8,128)S(1)} %reduce_sum.100), channel_id=1, replica_groups=mesh['dp'=8,'ta'=16,'ha'=4] {'ha'}, use_global_device_ids=true, to_apply=%region_16.17 | all-reduce | flops 1024 | bytes 8192 | tf_op jit(solution)/shard_map/psum | solution.py:54
  120.2 1.9 %collective-permute-start.1 = (bf16[2,4,2,384]{3,2,1,0:T(2,128)(2,1)S(1)}, bf16[2,4,2,384]{3,2,1,0:T(2,128)(2,1)S(1)}, u32[]{:S(2)}, u32[]{:S(2)}) collective-permute-start(bf16[2,4,2,384]{3,2,1,0:T(2,128)(2,1)S(1)} %slice.129), channel_id=1, source_target_pairs={{0,4},{4,8},{8,12},{12,16},{16,20},{20,24},{24,28},{28,32},{32,36}... | collective-permute-start | bytes 36872 | tf_op jit(solution)/shard_map/ppermute | solution.py:16
  122.1 5.8 %collective-permute-done.1 = bf16[2,4,2,384]{3,2,1,0:T(2,128)(2,1)S(1)} collective-permute-done((bf16[2,4,2,384]{3,2,1,0:T(2,128)(2,1)S(1)}, bf16[2,4,2,384]{3,2,1,0:T(2,128)(2,1)S(1)}, u32[]{:S(2)}, u32[]{:S(2)}) %collective-permute-start.1) | collective-permute-done | bytes 12320 | tf_op jit(solution)/shard_map/ppermute | solution.py:16
  128.1 0.9 stack.8
  129.0 6.7 %all-to-all-start.3 = ((bf16[4,18,4,2,384]{4,2,3,1,0:T(4,128)(2,1)}), bf16[4,18,4,2,384]{4,2,3,1,0:T(4,128)(2,1)S(1)}, u32[]{:S(2)}, u32[]{:S(2)}) async-start(bf16[4,18,4,2,384]{4,2,3,1,0:T(4,128)(2,1)} %stack.8), calls=%async_computation.3 | async-start | bytes 884736 | tf_op jit(solution)/shard_map/all_to_all | solution.py:46
  135.6 1.4 copy.54
  137.4 0.8 dynamic_slice.11
  138.1 12.2 %all-to-all-done.3 = bf16[4,18,4,2,384]{4,2,3,1,0:T(4,128)(2,1)S(1)} async-done(((bf16[4,18,4,2,384]{4,2,3,1,0:T(4,128)(2,1)}), bf16[4,18,4,2,384]{4,2,3,1,0:T(4,128)(2,1)S(1)}, u32[]{:S(2)}, u32[]{:S(2)}) %all-to-all-start.3) | async-done | bytes 442400 | tf_op jit(solution)/shard_map/all_to_all | solution.py:46
  151.0 5.5 %fusion.5 = f32[16,18,4,9,96]{4,1,3,2,0:T(8,128)S(1)} fusion(bf16[9,96,1152,1,1]{2,1,0,4,3:T(8,128)(2,1)S(1)} %bitcast.95, bf16[16,18,4,384]{3,1,2,0:T(8,128)(2,1)S(1)} %get-tuple-element.19, bf16[16,18,4,384]{3,1,2,0:T(8,128)(2,1)S(1)} %get-tuple-element.18, bf16[16,18,4,384]{3,1,2,0:T(8,128)(2,1)S(1)} %get-tuple-element.17), kind=kOutput, calls=%fused_computation.7 | convolution fusion | flops 2301198336 | bytes 8626176 | tf_op jit(solution)/shard_map/dot_general | solution.py:73
  156.8 15.1 %all_to_all.43 = f32[16,16,2,96]{3,2,0,1:T(2,128)S(1)} all-to-all(f32[16,16,2,96]{3,2,0,1:T(2,128)S(1)} %copy.55), channel_id=1, replica_groups=mesh['dp'=8,'ta'=16,'ha'=4] {'ha'}, dimensions={1} | all-to-all | bytes 393216 | tf_op jit(solution)/shard_map/all_to_all | solution.py:179
  172.5 0.8 add_convert_fusion
  (81 shorter events, 10.9 us)
Async XLA Ops:
  0.0 1.3 copy-start
  2.2 24.7 %all-to-all-start = ((bf16[64,2,768]{2,1,0:T(2,128)(2,1)}), bf16[64,2,768]{2,1,0:T(2,128)(2,1)S(1)}, u32[]{:S(2)}, u32[]{:S(2)}) async-start(bf16[64,2,768]{2,1,0:T(2,128)(2,1)} %reshape.367), calls=%async_computation | async-start | bytes 393216 | tf_op jit(solution)/shard_map/all_to_all | solution.py:113
  29.5 20.3 %copy-start.2 = (f32[384]{0:T(512)S(1)}, f32[384]{0:T(512)}, u32[]{:S(2)}) copy-start(f32[384]{0:T(512)} %param.15) | copy-start | bytes 4612
  29.5 20.3 %copy-start.3 = (f32[384]{0:T(512)S(1)}, f32[384]{0:T(512)}, u32[]{:S(2)}) copy-start(f32[384]{0:T(512)} %param.14) | copy-start | bytes 4612
  29.6 23.0 %copy-start.6 = (s32[6]{0:T(128)S(1)}, s32[6]{0:T(128)}, u32[]{:S(2)}) copy-start(s32[6]{0:T(128)} %param.13) | copy-start | bytes 76
  50.1 7.7 %collective-permute-start = (bf16[2,4,2,384]{3,2,1,0:T(2,128)(2,1)S(1)}, bf16[2,4,2,384]{3,2,1,0:T(2,128)(2,1)S(1)}, u32[]{:S(2)}, u32[]{:S(2)}) collective-permute-start(bf16[2,4,2,384]{3,2,1,0:T(2,128)(2,1)S(1)} %slice.119), channel_id=1, source_target_pairs={{0,4},{4,8},{8,12},{12,16},{16,20},{20,24},{24,28},{28,32},{32,36}... | collective-permute-start | bytes 36872 | tf_op jit(solution)/shard_map/ppermute | solution.py:16
  58.9 21.8 %all-to-all-start.1 = ((bf16[4,18,4,2,384]{4,2,3,1,0:T(4,128)(2,1)}), bf16[4,18,4,2,384]{4,2,3,1,0:T(4,128)(2,1)S(1)}, u32[]{:S(2)}, u32[]{:S(2)}) async-start(bf16[4,18,4,2,384]{4,2,3,1,0:T(4,128)(2,1)} %stack.6), calls=%async_computation.1 | async-start | bytes 884736 | tf_op jit(solution)/shard_map/all_to_all | solution.py:46
  99.5 20.3 %copy-start.4 = (f32[384]{0:T(512)S(1)}, f32[384]{0:T(512)}, u32[]{:S(2)}) copy-start(f32[384]{0:T(512)} %param.19) | copy-start | bytes 4612
  99.5 20.4 %copy-start.5 = (f32[384]{0:T(512)S(1)}, f32[384]{0:T(512)}, u32[]{:S(2)}) copy-start(f32[384]{0:T(512)} %param.18) | copy-start | bytes 4612
  119.0 16.6 %copy-start.1 = (bf16[3,3,3,96,384]{4,3,2,1,0:T(8,128)(2,1)S(1)}, bf16[3,3,3,96,384]{4,3,2,1,0:T(8,128)(2,1)}, u32[]{:S(2)}) copy-start(bf16[3,3,3,96,384]{4,3,2,1,0:T(8,128)(2,1)} %param.20) | copy-start | bytes 5971972
  120.2 7.7 %collective-permute-start.1 = (bf16[2,4,2,384]{3,2,1,0:T(2,128)(2,1)S(1)}, bf16[2,4,2,384]{3,2,1,0:T(2,128)(2,1)S(1)}, u32[]{:S(2)}, u32[]{:S(2)}) collective-permute-start(bf16[2,4,2,384]{3,2,1,0:T(2,128)(2,1)S(1)} %slice.129), channel_id=1, source_target_pairs={{0,4},{4,8},{8,12},{12,16},{16,20},{20,24},{24,28},{28,32},{32,36}... | collective-permute-start | bytes 36872 | tf_op jit(solution)/shard_map/ppermute | solution.py:16
  129.0 21.3 %all-to-all-start.3 = ((bf16[4,18,4,2,384]{4,2,3,1,0:T(4,128)(2,1)}), bf16[4,18,4,2,384]{4,2,3,1,0:T(4,128)(2,1)S(1)}, u32[]{:S(2)}, u32[]{:S(2)}) async-start(bf16[4,18,4,2,384]{4,2,3,1,0:T(4,128)(2,1)} %stack.8), calls=%async_computation.3 | async-start | bytes 884736 | tf_op jit(solution)/shard_map/all_to_all | solution.py:46
